TPU v7x, 256 devices: a whole 4x4x8 slice. The times are simulated.
256 devices in a mesh: row: 32 (over z, x), col: 8 (over y, core).
Axes of the slice: x: 4, y: 4, z: 8, core: 2. Of those that a mesh axis runs over, the one named last changes fastest.
Arguments:
- vectors: bfloat16 [256, 65536], P('col', 'row'), may hold values from -6 to 6
- hblocks: bfloat16 [1024, 12, 4096], P('row'), may hold values from -0.15625 to 0.15625
- counts: int32 [1024], P('row'), may hold values from 3 to 12, as said below
- sources: int32 [1024, 12], P('row'), may hold values from 0 to 95, as said below
- send_rows: int32 [2048], P('row'), may hold values from 0 to 31
Outputs:
- filtered: bfloat16 [256, 65536], P('col', 'row')
- gram_matrix: float32 [256, 256], P(None, 'col')
- projected: float32 [256, 256], P(None, 'col')
Inputs may be any that keep to these rules, and one draw needn't show every extreme that they name: Blocks 0 to counts[i] - 1 of block row i are live; the rows of every device include one with 12 live blocks. `sources`: entry 0 of block row i is i's own index within its device. On every device each slot value 32 + s, s below 64, stands exactly once, at block 1 or 2 of some row. `send_rows`: entries p * 64 + q * 2 + c name block rows of device p within it.
All inputs are finite; a program needn't handle non-finite values.
Results may differ from a plain program's by a relative error of at most 0.017.
Values may be sent and summed in bfloat16 or wider, within the bound.
No kernel may reach another device: no remote copies, remote signals or barrier semaphores. Data moves between devices by JAX's collectives and lax.ppermute only.
A program may use at most 128 MiB of HBM per device.

v0:
```python
import jax
import jax.numpy as jnp
from jax import lax
from jax.sharding import PartitionSpec as P

B = 64
K = 12
center_value = 0.25
half_width = 1.5


def on_device(vectors, hblocks, counts, sources, send_rows):
    rows_here = hblocks.shape[0]
    cols_here = vectors.shape[0]
    slots = send_rows.shape[0]
    live_mask = lax.broadcasted_iota(jnp.int32, (rows_here, K), 1) < counts[:, None]
    masked = jnp.where(live_mask[:, :, None], hblocks, jnp.zeros((), jnp.bfloat16)).reshape(
        rows_here, K, B, B
    )
    flat_sources = sources.reshape(-1)
    slot_table = lax.all_gather(send_rows, "row", axis=0, tiled=True)
    device_row = lax.axis_index("row")
    capacity = slots // lax.axis_size("row")
    positions = jnp.arange(slots, dtype=jnp.int32)
    peer_index = positions // capacity
    global_rows = (
        peer_index * rows_here
        + slot_table[peer_index * slots + device_row * capacity + positions % capacity]
    )

    def apply_operator(block_vectors):
        whole_blocks = lax.all_gather(block_vectors, "row", axis=0, tiled=True)
        incoming = whole_blocks[global_rows]
        extended = jnp.concatenate([block_vectors, incoming], 0)
        picked = extended[flat_sources].reshape(rows_here, K, cols_here, B)
        upper_part = jnp.einsum(
            "ikmb,ikab->ima", picked, masked, preferred_element_type=jnp.float32
        )
        mirror = jnp.einsum(
            "ima,ikab->ikmb", block_vectors, masked, preferred_element_type=jnp.float32
        )
        spread = jax.ops.segment_sum(
            mirror.reshape(rows_here * K, cols_here, B),
            flat_sources,
            num_segments=rows_here + slots,
        )
        returned = lax.all_to_all(
            spread[rows_here:], "row", split_axis=0, concat_axis=0, tiled=True
        )
        back_sums = jax.ops.segment_sum(returned, send_rows, num_segments=rows_here)
        return upper_part + spread[:rows_here] + back_sums

    start_blocks = vectors.reshape(cols_here, rows_here, B).transpose(1, 0, 2)
    start_float = start_blocks.astype(jnp.float32)
    first_image = apply_operator(start_blocks)
    first_step = ((first_image - center_value * start_float) / half_width).astype(jnp.bfloat16)
    second_image = apply_operator(first_step)
    second_step = (
        2.0 * (second_image - center_value * first_step.astype(jnp.float32)) / half_width
        - start_float
    ).astype(jnp.bfloat16)
    image_blocks = apply_operator(second_step).astype(jnp.bfloat16)
    filtered = second_step.transpose(1, 0, 2).reshape(cols_here, rows_here * B)
    image_rows = image_blocks.transpose(1, 0, 2).reshape(cols_here, rows_here * B)
    contract = (((1,), (1,)), ((), ()))
    stacked = jnp.concatenate([filtered, image_rows], 0)
    partial_value = lax.dot_general(
        lax.all_gather(filtered, "col", axis=0, tiled=True),
        stacked,
        contract,
        preferred_element_type=jnp.float32,
    )
    partial_value = partial_value.reshape(partial_value.shape[0], 2, cols_here)
    totals = lax.psum(partial_value.astype(jnp.bfloat16), "row").astype(jnp.float32)
    return (filtered, totals[:, 0, :], totals[:, 1, :])


def solution(mesh):
    return jax.shard_map(
        on_device,
        mesh=mesh,
        in_specs=(P("col", "row"), P("row", None, None), P("row"), P("row", None), P("row")),
        out_specs=(P("col", "row"), P(None, "col"), P(None, "col")),
        check_vma=False,
    )
```

profile of v0, /device:TPU:16, one launch (start us, length us, event | category | flops | bytes accessed | tf_op | source)
XLA Modules:
  0.0 545.5 jit_solution(17651293404976288670)
XLA Ops:
  7.2 1.2 reshape.175
  8.4 0.8 copy.75
  10.7 2.2 broadcast_select_fusion
  12.8 7.9 %reshape.178 = bf16[32,12,64,64]{3,2,0,1:T(8,128)(2,1)} reshape(bf16[32,12,4096]{2,0,1:T(8,128)(2,1)S(1)} %broadcast_select_fusion) | data formatting | bytes 6291456 | tf_op jit(solution)/shard_map/reshape | solution.py:17
  20.8 6.4 %fusion = f32[32,12,64,32]{2,3,1,0:T(8,128)} fusion(bf16[32,12,64,64]{3,2,0,1:T(8,128)(2,1)} %reshape.178, bf16[32,32,64]{2,1,0:T(8,128)(2,1)S(1)} %reshape.175), kind=kOutput, calls=%fused_computation.14 | convolution fusion | flops 100663296 | bytes 6422528 | tf_op jit(solution)/shard_map/ima,ikab->ikmb/dot_general | solution.py:39
  27.4 34.4 %scatter_fusion = f32[96,32,64]{2,1,0:T(8,128)S(1)} fusion(f32[96,32,64]{2,1,0:T(8,128)S(1)} %broadcast.194.clone, s32[384]{0:T(512)S(1)} %reshape.244, f32[384,32,64]{2,1,0:T(8,128)} %bitcast.74), kind=kCustom, calls=%fused_computation.7 | custom fusion | flops 786432 | bytes 9438720 | tf_op jit(solution)/shard_map/scatter-add | solution.py:42
  61.9 1.5 reshape.308
  63.3 11.3 %all-to-all-start = ((f32[32,1,4096]{2,1,0:T(1,128)}), f32[32,1,4096]{2,1,0:T(1,128)S(1)}, u32[]{:S(2)}, u32[]{:S(2)}) async-start(f32[32,1,4096]{2,1,0:T(1,128)} %reshape.308), calls=%async_computation | async-start | bytes 1048576 | tf_op jit(solution)/shard_map/all_to_all | solution.py:47
  76.3 26.1 %all-reduce = s32[2048]{0:T(1024)S(1)} all-reduce(s32[2048]{0:T(1024)S(1)} %dynamic-update-slice), channel_id=1, replica_groups=mesh['row'=32,'col'=8] {'row'}, use_global_device_ids=true, to_apply=%add | all-reduce | flops 2048 | bytes 16384
  103.8 1.9 reduce.2
  105.7 1.4 reshape.309
  107.1 13.4 %all-gather.5.cloned.1.call-done = bf16[1024,32,64]{2,1,0:T(8,128)(2,1)} async-done(((bf16[32,32,64]{2,1,0:T(8,128)(2,1)}), bf16[1024,32,64]{2,1,0:T(8,128)(2,1)}) %all-gather.5.cloned.1.call-update) | async-done | bytes 4194320 | tf_op jit(solution)/shard_map/all_gather | solution.py:32
  120.5 4.8 gather_fusion.1
  125.3 1.2 pad_maximum_fusion
  126.5 3.2 gather_fusion.2
  129.7 5.6 %fusion.27 = f32[32,32,64]{2,1,0:T(8,128)S(1)} fusion(bf16[32,12,32,64]{3,2,1,0:T(8,128)(2,1)} %bitcast.78, bf16[32,12,64,64]{3,2,0,1:T(8,128)(2,1)} %reshape.178, f32[96,32,64]{2,1,0:T(8,128)S(1)} %scatter_fusion), kind=kOutput, calls=%fused_computation.31 | convolution fusion | flops 100728832 | bytes 5242880 | tf_op jit(solution)/shard_map/ikmb,ikab->ima/dot_general | solution.py:36
  135.3 3.2 scatter_fusion.1
  138.4 0.8 fusion.32
  139.5 6.4 %fusion.4 = f32[32,12,64,32]{2,3,1,0:T(8,128)} fusion(bf16[32,12,64,64]{3,2,0,1:T(8,128)(2,1)} %reshape.178, bf16[32,32,64]{2,1,0:T(8,128)(2,1)} %fusion.32), kind=kOutput, calls=%fused_computation.18 | convolution fusion | flops 100663296 | bytes 6422528 | tf_op jit(solution)/shard_map/ima,ikab->ikmb/dot_general | solution.py:39
  146.1 34.4 %scatter_fusion.2 = f32[96,32,64]{2,1,0:T(8,128)S(1)} fusion(f32[96,32,64]{2,1,0:T(8,128)S(1)} %broadcast.194.clone.1, s32[384]{0:T(512)S(1)} %reshape.244, f32[384,32,64]{2,1,0:T(8,128)} %bitcast.75), kind=kCustom, calls=%fused_computation.9 | custom fusion | flops 786432 | bytes 9438720 | tf_op jit(solution)/shard_map/scatter-add | solution.py:42
  180.6 1.0 slice.49
  181.6 1.9 reshape.310
  183.5 30.1 %all_to_all.15 = f32[32,1,4096]{2,1,0:T(1,128)S(1)} all-to-all(f32[32,1,4096]{2,1,0:T(1,128)S(1)} %reshape.310), channel_id=1, replica_groups=mesh['row'=32,'col'=8] {'row'}, dimensions={0} | all-to-all | bytes 1048576 | tf_op jit(solution)/shard_map/all_to_all | solution.py:47
  213.6 1.9 reduce.3
  215.5 1.4 reshape.311
  216.9 26.6 %all-gather.7.cloned.1.call-done = bf16[1024,32,64]{2,1,0:T(8,128)(2,1)} async-done(((bf16[32,32,64]{2,1,0:T(8,128)(2,1)}), bf16[1024,32,64]{2,1,0:T(8,128)(2,1)}) %all-gather.7.cloned.1.call-update) | async-done | bytes 4194320 | tf_op jit(solution)/shard_map/all_gather | solution.py:32
  243.5 4.0 gather_fusion.3
  247.8 3.2 gather_fusion.4
  250.9 5.5 %fusion.24 = f32[32,32,64]{2,1,0:T(8,128)S(1)} fusion(bf16[32,12,32,64]{3,2,1,0:T(8,128)(2,1)} %bitcast.79, bf16[32,12,64,64]{3,2,0,1:T(8,128)(2,1)} %reshape.178, f32[96,32,64]{2,1,0:T(8,128)S(1)} %scatter_fusion.2), kind=kOutput, calls=%fused_computation.30 | convolution fusion | flops 100728832 | bytes 5242880 | tf_op jit(solution)/shard_map/ikmb,ikab->ima/dot_general | solution.py:36
  256.4 6.1 %scatter_fusion.3 = f32[32,32,64]{2,1,0:T(8,128)S(1)} fusion(f32[32,32,64]{2,1,0:T(8,128)S(1)} %fusion.24, s32[64]{0:T(128)S(1)} %copy-done.6, f32[64,32,64]{2,1,0:T(8,128)} %reshape.311), kind=kCustom, calls=%fused_computation.10 | custom fusion | flops 131072 | bytes 1573120 | tf_op jit(solution)/shard_map/scatter-add | solution.py:50
  262.6 0.9 fusion.33
  263.5 6.4 %fusion.8 = f32[32,12,64,32]{2,3,1,0:T(8,128)} fusion(bf16[32,12,64,64]{3,2,0,1:T(8,128)(2,1)} %reshape.178, bf16[32,32,64]{2,1,0:T(8,128)(2,1)} %fusion.33), kind=kOutput, calls=%fused_computation.22 | convolution fusion | flops 100663296 | bytes 6422528 | tf_op jit(solution)/shard_map/ima,ikab->ikmb/dot_general | solution.py:39
  270.1 34.4 %scatter_fusion.4 = f32[96,32,64]{2,1,0:T(8,128)S(1)} fusion(f32[96,32,64]{2,1,0:T(8,128)S(1)} %broadcast.194, s32[384]{0:T(512)S(1)} %reshape.244, f32[384,32,64]{2,1,0:T(8,128)} %bitcast.73), kind=kCustom, calls=%fused_computation.11 | custom fusion | flops 786432 | bytes 9438720 | tf_op jit(solution)/shard_map/scatter-add | solution.py:42
  304.5 1.0 slice.51
  305.5 2.7 reshape.312
  308.2 7.1 %all-to-all-start.2 = ((f32[32,1,4096]{2,1,0:T(1,128)}), f32[32,1,4096]{2,1,0:T(1,128)S(1)}, u32[]{:S(2)}, u32[]{:S(2)}) async-start(f32[32,1,4096]{2,1,0:T(1,128)} %reshape.312), calls=%async_computation.2 | async-start | bytes 1048576 | tf_op jit(solution)/shard_map/all_to_all | solution.py:47
  315.7 0.9 reshape.182
  316.7 22.2 %all-to-all-done.2 = f32[32,1,4096]{2,1,0:T(1,128)S(1)} async-done(((f32[32,1,4096]{2,1,0:T(1,128)}), f32[32,1,4096]{2,1,0:T(1,128)S(1)}, u32[]{:S(2)}, u32[]{:S(2)}) %all-to-all-start.2) | async-done | bytes 524320 | tf_op jit(solution)/shard_map/all_to_all | solution.py:47
  338.9 1.9 reduce.4
  340.8 1.4 reshape.313
  342.2 25.9 %all-gather.11.cloned.1.call-done = bf16[1024,32,64]{2,1,0:T(8,128)(2,1)} async-done(((bf16[32,32,64]{2,1,0:T(8,128)(2,1)}), bf16[1024,32,64]{2,1,0:T(8,128)(2,1)}) %all-gather.11.cloned.1.call-update) | async-done | bytes 4194320 | tf_op jit(solution)/shard_map/all_gather | solution.py:32
  368.1 4.0 gather_fusion.5
  372.3 3.2 gather_fusion.6
  375.5 5.6 %fusion.21 = f32[32,32,64]{2,1,0:T(8,128)S(1)} fusion(bf16[32,12,32,64]{3,2,1,0:T(8,128)(2,1)} %bitcast.77, bf16[32,12,64,64]{3,2,0,1:T(8,128)(2,1)} %reshape.178, f32[96,32,64]{2,1,0:T(8,128)S(1)} %scatter_fusion.4), kind=kOutput, calls=%fused_computation.29 | convolution fusion | flops 100728832 | bytes 5242880 | tf_op jit(solution)/shard_map/ikmb,ikab->ima/dot_general | solution.py:36
  381.1 3.2 scatter_fusion.5
  384.7 8.9 %all-gather.9.cloned.1.call-done = bf16[256,2048]{1,0:T(8,128)(2,1)} async-done(((bf16[32,2048]{1,0:T(8,128)(2,1)}), bf16[256,2048]{1,0:T(8,128)(2,1)}) %all-gather.9.cloned.1.call-update) | async-done | bytes 1048592 | tf_op jit(solution)/shard_map/all_gather | solution.py:68
  393.6 1.7 convolution_convert_fusion
  395.2 143.1 %psum.7 = bf16[256,2,32]{0,2,1:T(8,128)(2,1)S(1)} all-reduce(bf16[256,2,32]{0,2,1:T(8,128)(2,1)S(1)} %bitcast.82), channel_id=1, replica_groups=mesh['row'=32,'col'=8] {'row'}, use_global_device_ids=true, to_apply=%region_6.7 | all-reduce | flops 16384 | bytes 65536 | tf_op jit(solution)/shard_map/psum | solution.py:74
  (52 shorter events, 6.6 us)
Async XLA Ops:
  7.2 113.4 %all-gather.5.cloned.1.call-start = ((), (), s32[]{:S(2)}) async-start(), calls=%async_computation.3 | async-start | bytes 8650752 | tf_op jit(solution)/shard_map/all_gather | solution.py:32
  27.4 47.5 %copy-start.7 = (u32[256]{0:T(256)S(1)}, u32[256]{0:T(256)}, u32[]{:S(2)}) copy-start(u32[256]{0:T(256)} %constant.65) | copy-start | bytes 3076
  27.4 48.7 %copy-start.6 = (s32[64]{0:T(128)S(1)}, s32[64]{0:T(128)}, u32[]{:S(2)}) copy-start(s32[64]{0:T(128)} %param.9) | copy-start | bytes 772
  61.8 63.5 %copy-start.4 = (bf16[32,32,64]{2,0,1:T(8,128)(2,1)S(1)}, bf16[32,32,64]{2,0,1:T(8,128)(2,1)}, u32[]{:S(2)}) copy-start(bf16[32,32,64]{2,0,1:T(8,128)(2,1)} %copy.75) | copy-start | bytes 393220
  63.3 40.0 %all-to-all-start = ((f32[32,1,4096]{2,1,0:T(1,128)}), f32[32,1,4096]{2,1,0:T(1,128)S(1)}, u32[]{:S(2)}, u32[]{:S(2)}) async-start(f32[32,1,4096]{2,1,0:T(1,128)} %reshape.308), calls=%async_computation | async-start | bytes 1048576 | tf_op jit(solution)/shard_map/all_to_all | solution.py:47
  74.6 168.9 %all-gather.7.cloned.1.call-start = ((), (), s32[]{:S(2)}) async-start(), calls=%async_computation.4 | async-start | bytes 8650752 | tf_op jit(solution)/shard_map/all_gather | solution.py:32
  129.7 5.6 %copy-start.3 = (f32[64,32,64]{2,1,0:T(8,128)S(1)}, f32[64,32,64]{2,1,0:T(8,128)}, u32[]{:S(2)}) copy-start(f32[64,32,64]{2,1,0:T(8,128)} %reshape.309) | copy-start | bytes 1572868
  139.3 228.8 %all-gather.11.cloned.1.call-start = ((), (), s32[]{:S(2)}) async-start(), calls=%async_computation.6 | async-start | bytes 8650752 | tf_op jit(solution)/shard_map/all_gather | solution.py:32
  180.6 67.0 %copy-start.1 = (bf16[32,32,64]{2,1,0:T(8,128)(2,1)S(1)}, bf16[32,32,64]{2,1,0:T(8,128)(2,1)}, u32[]{:S(2)}) copy-start(bf16[32,32,64]{2,1,0:T(8,128)(2,1)} %fusion.32) | copy-start | bytes 393220
  270.1 45.5 %copy-start = (bf16[32,32,64]{2,1,0:T(8,128)(2,1)S(1)}, bf16[32,32,64]{2,1,0:T(8,128)(2,1)}, u32[]{:S(2)}) copy-start(bf16[32,32,64]{2,1,0:T(8,128)(2,1)} %fusion.33) | copy-start | bytes 393220
  308.2 30.7 %all-to-all-start.2 = ((f32[32,1,4096]{2,1,0:T(1,128)}), f32[32,1,4096]{2,1,0:T(1,128)S(1)}, u32[]{:S(2)}, u32[]{:S(2)}) async-start(f32[32,1,4096]{2,1,0:T(1,128)} %reshape.312), calls=%async_computation.2 | async-start | bytes 1048576 | tf_op jit(solution)/shard_map/all_to_all | solution.py:47
  315.3 78.2 %all-gather.9.cloned.1.call-start = ((), (), s32[]{:S(2)}) async-start(), calls=%async_computation.5 | async-start | bytes 1179648 | tf_op jit(solution)/shard_map/all_gather | solution.py:68
  375.5 5.6 %copy-start.2 = (f32[64,32,64]{2,1,0:T(8,128)S(1)}, f32[64,32,64]{2,1,0:T(8,128)}, u32[]{:S(2)}) copy-start(f32[64,32,64]{2,1,0:T(8,128)} %reshape.313) | copy-start | bytes 1572868
  375.5 18.1 %copy-start.5 = (bf16[32,2048]{1,0:T(8,128)(2,1)S(1)}, bf16[32,2048]{1,0:T(8,128)(2,1)}, u32[]{:S(2)}) copy-start(bf16[32,2048]{1,0:T(8,128)(2,1)} %reshape.182) | copy-start | bytes 393220
Sparse Core Ops, SparseCore 0:
  10.6 109.8 all-gather.4
  139.4 104.0 all-gather.6
  263.6 104.4 all-gather.10
  370.4 23.1 all-gather.8
where the time goes:
time: 549 us; the launch traced here: 546 us
  blocking collectives  199 us (36%)
  other arithmetic  127 us (23%)
  waiting for transfers between devices  97.1 us (18%)
  local copies, waits for them, and re-layouts  50.4 us (9%)
  matrix products  37.5 us (7%)
  starting transfers between devices  19 us (3%)
  between operations  14.8 us (3%)
    psum x1, blocking collectives, on_device(): lax.psum(partial_value.astype(jnp.bfloat16), 'row').astype(jnp.float32)  143 us
    scatter-add x3, other arithmetic, apply_operator(): jax.ops.segment_sum(mirror.reshape(rows_here * K, cols_here, B), flat_sou...  103 us
    all_gather x3, waiting for transfers between devices, apply_operator(): whole_blocks = lax.all_gather(block_vectors, 'row', axis=0, tiled=True)  65.9 us
    all_to_all x1, blocking collectives, apply_operator(): lax.all_to_all(spread[rows_here:], 'row', split_axis=0, concat_axis=0, ti...  30.1 us
    unnamed x1, blocking collectives  26.1 us
    all_to_all x2, waiting for transfers between devices, apply_operator(): lax.all_to_all(spread[rows_here:], 'row', split_axis=0, concat_axis=0, ti...  22.2 us
    dot_general x3, matrix products, apply_operator(): jnp.einsum('ima,ikab->ikmb', block_vectors, masked, preferred_element_typ...  19.2 us
    all_to_all x2, starting transfers between devices, apply_operator(): lax.all_to_all(spread[rows_here:], 'row', split_axis=0, concat_axis=0, ti...  18.4 us
  transfers between devices with their start and end apart: 6, of which 5 were waited for; matrix products, arithmetic and copies ran while one was open for 32% of the time, Pallas kernels for 0%

commit v1 on v0

--- a/solution.py
+++ b/solution.py
@@ -71,7 +71,9 @@
         preferred_element_type=jnp.float32,
     )
     partial_value = partial_value.reshape(partial_value.shape[0], 2, cols_here)
-    totals = lax.psum(partial_value.astype(jnp.bfloat16), "row").astype(jnp.float32)
+    totals = jnp.sum(lax.all_gather(partial_value.astype(jnp.bfloat16), "row"), axis=0).astype(
+        jnp.float32
+    )
     return (filtered, totals[:, 0, :], totals[:, 1, :])
 
 

time: 549 us -> 486 us (0.89)
  blocking collectives: 199 us -> 56.2 us
  waiting for transfers between devices: 97.1 us -> 175 us
    psum x1 -> x0, blocking collectives: 143 us -> none  [on_device(): lax.psum(partial_value.astype(jnp.bfloat16), 'row').astype(jnp.float32)]
    all_gather x0 -> x1, waiting for transfers between devices: none -> 78.1 us  [on_device(): lax.all_gather(partial_value.astype(jnp.bfloat16), 'row')]
  transfers between devices with their start and end apart: 6 -> 7, of which waited for: 5 -> 6; matrix products, arithmetic and copies ran while one was open for 32% -> 36% of each run, Pallas kernels for 0% -> 0%
where the time goes in v1:
time: 486 us; the launch traced here: 483 us
  waiting for transfers between devices  175 us (36%)
  other arithmetic  129 us (27%)
  blocking collectives  56.2 us (12%)
  local copies, waits for them, and re-layouts  50.4 us (10%)
  matrix products  38.1 us (8%)
  starting transfers between devices  19 us (4%)
  between operations  14.8 us (3%)
    scatter-add x3, other arithmetic, apply_operator(): jax.ops.segment_sum(mirror.reshape(rows_here * K, cols_here, B), flat_sou...  103 us
    all_gather x1, waiting for transfers between devices, on_device(): lax.all_gather(partial_value.astype(jnp.bfloat16), 'row')  78.1 us
    all_gather x3, waiting for transfers between devices, apply_operator(): whole_blocks = lax.all_gather(block_vectors, 'row', axis=0, tiled=True)  65.9 us
    all_to_all x1, blocking collectives, apply_operator(): lax.all_to_all(spread[rows_here:], 'row', split_axis=0, concat_axis=0, ti...  30.1 us
    unnamed x1, blocking collectives  26.1 us
    all_to_all x2, waiting for transfers between devices, apply_operator(): lax.all_to_all(spread[rows_here:], 'row', split_axis=0, concat_axis=0, ti...  22.2 us
    dot_general x3, matrix products, apply_operator(): jnp.einsum('ima,ikab->ikmb', block_vectors, masked, preferred_element_typ...  19.2 us
    all_to_all x2, starting transfers between devices, apply_operator(): lax.all_to_all(spread[rows_here:], 'row', split_axis=0, concat_axis=0, ti...  18.4 us
  transfers between devices with their start and end apart: 7, of which 6 were waited for; matrix products, arithmetic and copies ran while one was open for 36% of the time, Pallas kernels for 0%

profile of v1, /device:TPU:16, one launch (start us, length us, event | category | flops | bytes accessed | tf_op | source)
XLA Modules:
  0.0 482.5 jit_solution(17144432173058607298)
XLA Ops:
  7.2 1.2 reshape.185
  10.7 2.2 broadcast_select_fusion
  12.8 7.9 %reshape.188 = bf16[32,12,64,64]{3,2,0,1:T(8,128)(2,1)} reshape(bf16[32,12,4096]{2,0,1:T(8,128)(2,1)S(1)} %broadcast_select_fusion) | data formatting | bytes 6291456 | tf_op jit(solution)/shard_map/reshape | solution.py:17
  20.8 6.4 %fusion = f32[32,12,64,32]{2,3,1,0:T(8,128)} fusion(bf16[32,12,64,64]{3,2,0,1:T(8,128)(2,1)} %reshape.188, bf16[32,32,64]{2,1,0:T(8,128)(2,1)S(1)} %reshape.185), kind=kOutput, calls=%fused_computation.14 | convolution fusion | flops 100663296 | bytes 6422528 | tf_op jit(solution)/shard_map/ima,ikab->ikmb/dot_general | solution.py:39
  27.4 34.4 %scatter_fusion = f32[96,32,64]{2,1,0:T(8,128)S(1)} fusion(f32[96,32,64]{2,1,0:T(8,128)S(1)} %broadcast.194.clone, s32[384]{0:T(512)S(1)} %reshape.254, f32[384,32,64]{2,1,0:T(8,128)} %bitcast.74), kind=kCustom, calls=%fused_computation.7 | custom fusion | flops 786432 | bytes 9438720 | tf_op jit(solution)/shard_map/scatter-add | solution.py:42
  61.9 1.5 reshape.318
  63.3 11.3 %all-to-all-start = ((f32[32,1,4096]{2,1,0:T(1,128)}), f32[32,1,4096]{2,1,0:T(1,128)S(1)}, u32[]{:S(2)}, u32[]{:S(2)}) async-start(f32[32,1,4096]{2,1,0:T(1,128)} %reshape.318), calls=%async_computation | async-start | bytes 1048576 | tf_op jit(solution)/shard_map/all_to_all | solution.py:47
  76.3 26.1 %all-reduce = s32[2048]{0:T(1024)S(1)} all-reduce(s32[2048]{0:T(1024)S(1)} %dynamic-update-slice), channel_id=1, replica_groups=mesh['row'=32,'col'=8] {'row'}, use_global_device_ids=true, to_apply=%add | all-reduce | flops 2048 | bytes 16384
  103.8 1.9 reduce.3
  105.7 1.4 reshape.319
  107.1 13.4 %all-gather.6.cloned.1.call-done = bf16[1024,32,64]{2,1,0:T(8,128)(2,1)} async-done(((bf16[32,32,64]{2,1,0:T(8,128)(2,1)}), bf16[1024,32,64]{2,1,0:T(8,128)(2,1)}) %all-gather.6.cloned.1.call-update) | async-done | bytes 4194320 | tf_op jit(solution)/shard_map/all_gather | solution.py:32
  120.5 4.8 gather_fusion.1
  125.3 1.2 pad_maximum_fusion
  126.5 3.2 gather_fusion.2
  129.7 5.6 %fusion.27 = f32[32,32,64]{2,1,0:T(8,128)S(1)} fusion(bf16[32,12,32,64]{3,2,1,0:T(8,128)(2,1)} %bitcast.78, bf16[32,12,64,64]{3,2,0,1:T(8,128)(2,1)} %reshape.188, f32[96,32,64]{2,1,0:T(8,128)S(1)} %scatter_fusion), kind=kOutput, calls=%fused_computation.31 | convolution fusion | flops 100728832 | bytes 5242880 | tf_op jit(solution)/shard_map/ikmb,ikab->ima/dot_general | solution.py:36
  135.3 3.2 scatter_fusion.1
  138.4 0.8 fusion.32
  139.5 6.4 %fusion.4 = f32[32,12,64,32]{2,3,1,0:T(8,128)} fusion(bf16[32,12,64,64]{3,2,0,1:T(8,128)(2,1)} %reshape.188, bf16[32,32,64]{2,1,0:T(8,128)(2,1)} %fusion.32), kind=kOutput, calls=%fused_computation.18 | convolution fusion | flops 100663296 | bytes 6422528 | tf_op jit(solution)/shard_map/ima,ikab->ikmb/dot_general | solution.py:39
  146.1 34.4 %scatter_fusion.2 = f32[96,32,64]{2,1,0:T(8,128)S(1)} fusion(f32[96,32,64]{2,1,0:T(8,128)S(1)} %broadcast.194.clone.1, s32[384]{0:T(512)S(1)} %reshape.254, f32[384,32,64]{2,1,0:T(8,128)} %bitcast.75), kind=kCustom, calls=%fused_computation.9 | custom fusion | flops 786432 | bytes 9438720 | tf_op jit(solution)/shard_map/scatter-add | solution.py:42
  180.6 1.0 slice.49
  181.6 1.9 reshape.320
  183.5 30.1 %all_to_all.15 = f32[32,1,4096]{2,1,0:T(1,128)S(1)} all-to-all(f32[32,1,4096]{2,1,0:T(1,128)S(1)} %reshape.320), channel_id=1, replica_groups=mesh['row'=32,'col'=8] {'row'}, dimensions={0} | all-to-all | bytes 1048576 | tf_op jit(solution)/shard_map/all_to_all | solution.py:47
  213.6 1.9 reduce.4
  215.5 1.4 reshape.321
  216.9 26.6 %all-gather.8.cloned.1.call-done = bf16[1024,32,64]{2,1,0:T(8,128)(2,1)} async-done(((bf16[32,32,64]{2,1,0:T(8,128)(2,1)}), bf16[1024,32,64]{2,1,0:T(8,128)(2,1)}) %all-gather.8.cloned.1.call-update) | async-done | bytes 4194320 | tf_op jit(solution)/shard_map/all_gather | solution.py:32
  243.5 4.0 gather_fusion.3
  247.8 3.2 gather_fusion.4
  250.9 5.5 %fusion.24 = f32[32,32,64]{2,1,0:T(8,128)S(1)} fusion(bf16[32,12,32,64]{3,2,1,0:T(8,128)(2,1)} %bitcast.79, bf16[32,12,64,64]{3,2,0,1:T(8,128)(2,1)} %reshape.188, f32[96,32,64]{2,1,0:T(8,128)S(1)} %scatter_fusion.2), kind=kOutput, calls=%fused_computation.30 | convolution fusion | flops 100728832 | bytes 5242880 | tf_op jit(solution)/shard_map/ikmb,ikab->ima/dot_general | solution.py:36
  256.4 6.1 %scatter_fusion.3 = f32[32,32,64]{2,1,0:T(8,128)S(1)} fusion(f32[32,32,64]{2,1,0:T(8,128)S(1)} %fusion.24, s32[64]{0:T(128)S(1)} %copy-done.6, f32[64,32,64]{2,1,0:T(8,128)} %reshape.321), kind=kCustom, calls=%fused_computation.10 | custom fusion | flops 131072 | bytes 1573120 | tf_op jit(solution)/shard_map/scatter-add | solution.py:50
  262.6 0.9 fusion.33
  263.5 6.4 %fusion.8 = f32[32,12,64,32]{2,3,1,0:T(8,128)} fusion(bf16[32,12,64,64]{3,2,0,1:T(8,128)(2,1)} %reshape.188, bf16[32,32,64]{2,1,0:T(8,128)(2,1)} %fusion.33), kind=kOutput, calls=%fused_computation.22 | convolution fusion | flops 100663296 | bytes 6422528 | tf_op jit(solution)/shard_map/ima,ikab->ikmb/dot_general | solution.py:39
  270.1 34.4 %scatter_fusion.4 = f32[96,32,64]{2,1,0:T(8,128)S(1)} fusion(f32[96,32,64]{2,1,0:T(8,128)S(1)} %broadcast.194, s32[384]{0:T(512)S(1)} %reshape.254, f32[384,32,64]{2,1,0:T(8,128)} %bitcast.73), kind=kCustom, calls=%fused_computation.11 | custom fusion | flops 786432 | bytes 9438720 | tf_op jit(solution)/shard_map/scatter-add | solution.py:42
  304.5 1.0 slice.51
  305.5 2.7 reshape.322
  308.2 7.1 %all-to-all-start.2 = ((f32[32,1,4096]{2,1,0:T(1,128)}), f32[32,1,4096]{2,1,0:T(1,128)S(1)}, u32[]{:S(2)}, u32[]{:S(2)}) async-start(f32[32,1,4096]{2,1,0:T(1,128)} %reshape.322), calls=%async_computation.2 | async-start | bytes 1048576 | tf_op jit(solution)/shard_map/all_to_all | solution.py:47
  315.5 0.9 reshape.192
  316.7 22.2 %all-to-all-done.2 = f32[32,1,4096]{2,1,0:T(1,128)S(1)} async-done(((f32[32,1,4096]{2,1,0:T(1,128)}), f32[32,1,4096]{2,1,0:T(1,128)S(1)}, u32[]{:S(2)}, u32[]{:S(2)}) %all-to-all-start.2) | async-done | bytes 524320 | tf_op jit(solution)/shard_map/all_to_all | solution.py:47
  338.9 1.9 reduce.5
  340.8 1.4 reshape.323
  342.2 25.9 %all-gather.12.cloned.1.call-done = bf16[1024,32,64]{2,1,0:T(8,128)(2,1)} async-done(((bf16[32,32,64]{2,1,0:T(8,128)(2,1)}), bf16[1024,32,64]{2,1,0:T(8,128)(2,1)}) %all-gather.12.cloned.1.call-update) | async-done | bytes 4194320 | tf_op jit(solution)/shard_map/all_gather | solution.py:32
  368.1 4.0 gather_fusion.5
  372.3 3.2 gather_fusion.6
  375.5 5.6 %fusion.21 = f32[32,32,64]{2,1,0:T(8,128)S(1)} fusion(bf16[32,12,32,64]{3,2,1,0:T(8,128)(2,1)} %bitcast.77, bf16[32,12,64,64]{3,2,0,1:T(8,128)(2,1)} %reshape.188, f32[96,32,64]{2,1,0:T(8,128)S(1)} %scatter_fusion.4), kind=kOutput, calls=%fused_computation.29 | convolution fusion | flops 100728832 | bytes 5242880 | tf_op jit(solution)/shard_map/ikmb,ikab->ima/dot_general | solution.py:36
  381.1 3.2 scatter_fusion.5
  384.7 8.9 %all-gather.10.cloned.1.call-done = bf16[256,2048]{1,0:T(8,128)(2,1)} async-done(((bf16[32,2048]{1,0:T(8,128)(2,1)}), bf16[256,2048]{1,0:T(8,128)(2,1)}) %all-gather.10.cloned.1.call-update) | async-done | bytes 1048592 | tf_op jit(solution)/shard_map/all_gather | solution.py:68
  393.6 2.3 convolution_convert_fusion
  395.9 78.1 %all-gather.14.cloned.1.call-done = bf16[32,256,2,32]{1,3,2,0:T(8,128)(2,1)} async-done(((bf16[1,256,2,32]{1,3,2,0:T(8,128)(2,1)}), bf16[32,256,2,32]{1,3,2,0:T(8,128)(2,1)}) %all-gather.14.cloned.1.call-update) | async-done | bytes 1048592 | tf_op jit(solution)/shard_map/all_gather | solution.py:74
  474.0 1.4 reduce_sum.12
  (55 shorter events, 7.5 us)
Async XLA Ops:
  7.2 113.4 %all-gather.6.cloned.1.call-start = ((), (), s32[]{:S(2)}) async-start(), calls=%async_computation.3 | async-start | bytes 8650752 | tf_op jit(solution)/shard_map/all_gather | solution.py:32
  27.4 47.5 %copy-start.7 = (u32[256]{0:T(256)S(1)}, u32[256]{0:T(256)}, u32[]{:S(2)}) copy-start(u32[256]{0:T(256)} %constant.67) | copy-start | bytes 3076
  27.4 48.7 %copy-start.6 = (s32[64]{0:T(128)S(1)}, s32[64]{0:T(128)}, u32[]{:S(2)}) copy-start(s32[64]{0:T(128)} %param.9) | copy-start | bytes 772
  61.8 63.5 %copy-start.4 = (bf16[32,32,64]{2,0,1:T(8,128)(2,1)S(1)}, bf16[32,32,64]{2,0,1:T(8,128)(2,1)}, u32[]{:S(2)}) copy-start(bf16[32,32,64]{2,0,1:T(8,128)(2,1)} %copy.75) | copy-start | bytes 393220
  63.3 40.0 %all-to-all-start = ((f32[32,1,4096]{2,1,0:T(1,128)}), f32[32,1,4096]{2,1,0:T(1,128)S(1)}, u32[]{:S(2)}, u32[]{:S(2)}) async-start(f32[32,1,4096]{2,1,0:T(1,128)} %reshape.318), calls=%async_computation | async-start | bytes 1048576 | tf_op jit(solution)/shard_map/all_to_all | solution.py:47
  74.6 168.9 %all-gather.8.cloned.1.call-start = ((), (), s32[]{:S(2)}) async-start(), calls=%async_computation.4 | async-start | bytes 8650752 | tf_op jit(solution)/shard_map/all_gather | solution.py:32
  129.7 5.6 %copy-start.3 = (f32[64,32,64]{2,1,0:T(8,128)S(1)}, f32[64,32,64]{2,1,0:T(8,128)}, u32[]{:S(2)}) copy-start(f32[64,32,64]{2,1,0:T(8,128)} %reshape.319) | copy-start | bytes 1572868
  139.3 228.8 %all-gather.12.cloned.1.call-start = ((), (), s32[]{:S(2)}) async-start(), calls=%async_computation.6 | async-start | bytes 8650752 | tf_op jit(solution)/shard_map/all_gather | solution.py:32
  180.6 67.0 %copy-start.1 = (bf16[32,32,64]{2,1,0:T(8,128)(2,1)S(1)}, bf16[32,32,64]{2,1,0:T(8,128)(2,1)}, u32[]{:S(2)}) copy-start(bf16[32,32,64]{2,1,0:T(8,128)(2,1)} %fusion.32) | copy-start | bytes 393220
  270.1 45.3 %copy-start = (bf16[32,32,64]{2,1,0:T(8,128)(2,1)S(1)}, bf16[32,32,64]{2,1,0:T(8,128)(2,1)}, u32[]{:S(2)}) copy-start(bf16[32,32,64]{2,1,0:T(8,128)(2,1)} %fusion.33) | copy-start | bytes 393220
  308.2 30.7 %all-to-all-start.2 = ((f32[32,1,4096]{2,1,0:T(1,128)}), f32[32,1,4096]{2,1,0:T(1,128)S(1)}, u32[]{:S(2)}, u32[]{:S(2)}) async-start(f32[32,1,4096]{2,1,0:T(1,128)} %reshape.322), calls=%async_computation.2 | async-start | bytes 1048576 | tf_op jit(solution)/shard_map/all_to_all | solution.py:47
  315.3 78.2 %all-gather.10.cloned.1.call-start = ((), (), s32[]{:S(2)}) async-start(), calls=%async_computation.5 | async-start | bytes 1179648 | tf_op jit(solution)/shard_map/all_gather | solution.py:68
  316.5 157.5 %all-gather.14.cloned.1.call-start = ((), (), s32[]{:S(2)}) async-start(), calls=%async_computation.7 | async-start | bytes 1081344 | tf_op jit(solution)/shard_map/all_gather | solution.py:74
  375.5 5.6 %copy-start.2 = (f32[64,32,64]{2,1,0:T(8,128)S(1)}, f32[64,32,64]{2,1,0:T(8,128)}, u32[]{:S(2)}) copy-start(f32[64,32,64]{2,1,0:T(8,128)} %reshape.323) | copy-start | bytes 1572868
  375.5 18.1 %copy-start.5 = (bf16[32,2048]{1,0:T(8,128)(2,1)S(1)}, bf16[32,2048]{1,0:T(8,128)(2,1)}, u32[]{:S(2)}) copy-start(bf16[32,2048]{1,0:T(8,128)(2,1)} %reshape.192) | copy-start | bytes 393220
Sparse Core Ops, SparseCore 0:
  10.6 109.8 all-gather.5
  139.4 104.0 all-gather.7
  263.6 104.4 all-gather.11
  370.4 23.1 all-gather.9
  396.6 77.3 all-gather.13
